TPU v7x, 32 devices: a whole 2x2x4 slice. The times are simulated.
32 devices in a mesh: lon: 16 (over z, x, core), lat: 2 (over y).
Axes of the slice: x: 2, y: 2, z: 4, core: 2. Of those that a mesh axis runs over, the one named last changes fastest.
Arguments:
- tracer_start: float32 [3, 16, 32, 2048], P(None, None, 'lat', 'lon'), may hold values from -6 to 6
- source: float32 [3, 16, 32, 2048], P(None, None, 'lat', 'lon'), may hold values from -3 to 3
- target: float32 [3, 16, 32, 2048], P(None, None, 'lat', 'lon'), may hold values from -27 to 27
- east_vel: float32 [16, 32, 2048], P(None, 'lat', 'lon'), may hold values from -0.12 to 0.12
- north_vel: float32 [16, 32, 2048], P(None, 'lat', 'lon'), may hold values from -0.12 to 0.12
- vertical_vel: float32 [16, 32, 2048], P(None, 'lat', 'lon'), may hold values from -0.12 to 0.12
- diffusivity: float32 [16, 32, 2048], P(None, 'lat', 'lon'), may hold values from 0.01 to 0.04
- sea_mask: int32 [16, 32, 2048], P(None, 'lat', 'lon'), may hold values 0 or 1
- reaction_rate: float32 [3, 16], replicated, may hold values from 0.05 to 0.5
- fold_partner: int32 [2048], P('lon'), may hold values from 0 to 2047, as said below
Outputs:
- source_grad: float32 [3, 16, 32, 2048], P(None, None, 'lat', 'lon')
- grad_norm: float32 [], replicated
Inputs may be any that keep to these rules, and one draw needn't show every extreme that they name: fold_partner[fold_partner[i]] = i; column i meets column (s - i) mod 2048 across the fold, for one s of each draw.
All inputs are finite; a program needn't handle non-finite values. No bound on the sum of `sea_mask` on one device may be relied on, other than what follows from the above.
Results may differ from a plain program's by a relative error of at most 0.00002.
Values sent between devices are 32-bit elements; how exact they have to be, the bound alone decides.
A program may use at most 64 MiB of HBM per device.

v0:
```python
import jax
import jax.numpy as jnp
from jax import lax
from jax.sharding import PartitionSpec as P

STEPS = 4


def with_halo(block, sides, width, periodic):
    for axis, dim in sides:
        count = lax.axis_size(axis)
        forward = [(i, i + 1) for i in range(count - 1)]
        if periodic:
            forward.append((count - 1, 0))
        backward = [(target, source) for source, target in forward]
        low = lax.ppermute(
            lax.slice_in_dim(block, block.shape[dim] - width, None, axis=dim), axis, forward
        )
        high = lax.ppermute(lax.slice_in_dim(block, 0, width, axis=dim), axis, backward)
        block = jnp.concatenate([low, block, high], axis=dim)
    return block


def upwind_pair(velocity, mixing, face_sea):
    flow_rate = velocity * face_sea
    mixing_part = mixing * face_sea
    return (jnp.maximum(flow_rate, 0.0) + mixing_part, jnp.minimum(flow_rate, 0.0) - mixing_part)


def on_device(
    tracer_start,
    source,
    target,
    east_vel,
    north_vel,
    vertical_vel,
    diffusivity,
    sea_mask,
    reaction_rate,
    fold_partner,
):
    ocean = sea_mask.astype(jnp.float32)
    statics = jnp.stack([east_vel, north_vel, diffusivity, ocean])
    wide_static = with_halo(statics, (("lon", 3),), 1, True)
    tall_static = with_halo(statics, (("lat", 2),), 1, False)
    west_cell = wide_static[..., :-1]
    east_cell = wide_static[..., 1:]
    east_own, east_next = upwind_pair(
        west_cell[0], 0.5 * (west_cell[2] + east_cell[2]), west_cell[3] * east_cell[3]
    )
    below_row = tall_static[:, :, :-1, :]
    above_row = tall_static[:, :, 1:, :]
    north_own, north_next = upwind_pair(
        below_row[1], 0.5 * (below_row[2] + above_row[2]), below_row[3] * above_row[3]
    )
    up_own, up_next = upwind_pair(
        vertical_vel[:-1], 0.5 * (diffusivity[:-1] + diffusivity[1:]), ocean[:-1] * ocean[1:]
    )
    top_static = jnp.stack([north_vel[:, -1, :], diffusivity[:, -1, :], ocean[:, -1, :]])
    fold_all = lax.all_gather(top_static, "lon", axis=2, tiled=True)
    across = jnp.take(fold_all, fold_partner, axis=2)
    north_top = (lax.axis_index("lat") == lax.axis_size("lat") - 1).astype(jnp.float32)
    fold_own, fold_next = upwind_pair(
        0.5 * (top_static[0] - across[0]),
        0.5 * (top_static[1] + across[1]),
        top_static[2] * across[2] * north_top,
    )
    decay_rate = reaction_rate[:, :, None, None]

    def neighbours(quantity):
        east_west = with_halo(quantity, (("lon", 3),), 1, True)
        south_north = with_halo(quantity, (("lat", 2),), 1, False)
        top_row = quantity[:, :, -1, :]
        whole_top = lax.all_gather(top_row, "lon", axis=2, tiled=True)
        partner_row = jnp.take(whole_top, fold_partner, axis=2)
        return (east_west, south_north, partner_row)

    kept_states = [tracer_start]
    for repeat in range(STEPS):
        advance_quantity = kept_states[-1]
        uptake = decay_rate * advance_quantity / jnp.sqrt(1.0 + advance_quantity * advance_quantity)
        divergence_east_west, divergence_south_north, divergence_partner_row = neighbours(
            advance_quantity
        )
        east_flux = (
            east_own * divergence_east_west[..., :-1] + east_next * divergence_east_west[..., 1:]
        )
        north_flux = (
            north_own * divergence_south_north[:, :, :-1, :]
            + north_next * divergence_south_north[:, :, 1:, :]
        )
        divergence_top_row = advance_quantity[:, :, -1, :]
        fold_flux = fold_own * divergence_top_row + fold_next * divergence_partner_row
        north_flux = north_flux.at[:, :, -1, :].add(fold_flux)
        up_flux = up_own * advance_quantity[:, :-1] + up_next * advance_quantity[:, 1:]
        zero_level = jnp.zeros_like(advance_quantity[:, :1])
        vertical_part = jnp.concatenate([up_flux, zero_level], 1) - jnp.concatenate(
            [zero_level, up_flux], 1
        )
        kept_states.append(
            ocean
            * (
                advance_quantity
                - (
                    east_flux[..., 1:]
                    - east_flux[..., :-1]
                    + (north_flux[:, :, 1:, :] - north_flux[:, :, :-1, :])
                    + vertical_part
                )
                - uptake
                + source
            )
        )
    last_state = kept_states[-1]
    adjoint = ocean * (last_state - target)
    source_grad = ocean * adjoint
    for backward in range(STEPS - 1, 0, -1):
        current = kept_states[backward]
        weight = ocean * adjoint
        transposed_east_west, transposed_south_north, transposed_partner_row = neighbours(weight)
        east_diff = transposed_east_west[..., :-1] - transposed_east_west[..., 1:]
        north_diff = transposed_south_north[:, :, :-1, :] - transposed_south_north[:, :, 1:, :]
        up_diff = weight[:, :-1] - weight[:, 1:]
        result = east_own[..., 1:] * east_diff[..., 1:] + east_next[..., :-1] * east_diff[..., :-1]
        result = result + (
            north_own[:, 1:, :] * north_diff[:, :, 1:, :]
            + north_next[:, :-1, :] * north_diff[:, :, :-1, :]
        )
        result = result.at[:, :, -1, :].add(
            fold_own * (weight[:, :, -1, :] - transposed_partner_row)
        )
        transposed_zero_level = jnp.zeros_like(weight[:, :1])
        result = result + (
            jnp.concatenate([up_own * up_diff, transposed_zero_level], 1)
            + jnp.concatenate([transposed_zero_level, up_next * up_diff], 1)
        )
        spread = 1.0 + current * current
        adjoint = weight - result - decay_rate / (spread * jnp.sqrt(spread)) * weight
        source_grad = source_grad + ocean * adjoint
    squares = lax.psum(jnp.sum(source_grad * source_grad), ("lon", "lat"))
    return (source_grad, jnp.sqrt(squares))


def solution(mesh):
    return jax.shard_map(
        on_device,
        mesh=mesh,
        in_specs=(
            P(None, None, "lat", "lon"),
            P(None, None, "lat", "lon"),
            P(None, None, "lat", "lon"),
            P(None, "lat", "lon"),
            P(None, "lat", "lon"),
            P(None, "lat", "lon"),
            P(None, "lat", "lon"),
            P(None, "lat", "lon"),
            P(),
            P("lon"),
        ),
        out_specs=(P(None, None, "lat", "lon"), P()),
        check_vma=False,
    )
```

profile of v0, /device:TPU:0, one launch (start us, length us, event | category | flops | bytes accessed | tf_op | source)
XLA Modules:
  0.0 427.2 jit_solution(13991767795987144747)
XLA Ops:
  3.3 5.5 %collective-permute-start.6 = (f32[3,16,1,128]{3,1,0,2:T(8,128)}, f32[3,16,1,128]{3,1,0,2:T(8,128)}, u32[]{:S(2)}, u32[]{:S(2)}) collective-permute-start(f32[3,16,1,128]{3,1,0,2:T(8,128)} %get-tuple-element.160), channel_id=1, source_target_pairs={{0,1},{2,3},{4,5},{6,7},{8,9},{10,11},{12,13},{14,15},{16,17},{18,... | collective-permute-start | bytes 73736 | tf_op jit(solution)/shard_map/ppermute | solution.py:16
  20.2 23.5 %all_gather.24 = f32[3,16,2048]{2,1,0:T(8,128)S(1)} all-gather(f32[3,16,128]{2,1,0:T(8,128)S(1)} %pad_maximum_fusion.12), channel_id=1, replica_groups=mesh['lon'=16,'lat'=2] {'lon'}, dimensions={2}, use_global_device_ids=true | all-gather | bytes 417792 | tf_op jit(solution)/shard_map/all_gather | solution.py:60
  50.7 19.9 %all-gather = f32[3,16,1,2048]{3,1,2,0:T(8,128)S(1)} all-gather(f32[3,16,1,128]{3,1,2,0:T(8,128)S(1)} %get-tuple-element.158), channel_id=2, replica_groups=mesh['lon'=16,'lat'=2] {'lon'}, dimensions={3}, use_global_device_ids=true | all-gather | bytes 417792 | tf_op jit(solution)/shard_map/all_gather | solution.py:74
  88.6 5.7 %collective-permute-start.4 = (f32[4,16,1,128]{3,2,1,0:T(1,128)}, f32[4,16,1,128]{3,2,1,0:T(1,128)S(1)}, u32[]{:S(2)}, u32[]{:S(2)}) collective-permute-start(f32[4,16,1,128]{3,2,1,0:T(1,128)} %get-tuple-element.118), channel_id=1, source_target_pairs={{0,1},{2,3},{4,5},{6,7},{8,9},{10,11},{12,13},{14,15},{16,17},{18,... | collective-permute-start | bytes 98312 | tf_op jit(solution)/shard_map/ppermute | solution.py:16
  101.0 4.7 %collective-permute-start.10 = (f32[3,16,1,128]{3,1,0,2:T(8,128)}, f32[3,16,1,128]{3,1,0,2:T(8,128)}, u32[]{:S(2)}, u32[]{:S(2)}) collective-permute-start(f32[3,16,1,128]{3,1,0,2:T(8,128)} %get-tuple-element.155), channel_id=1, source_target_pairs={{0,1},{2,3},{4,5},{6,7},{8,9},{10,11},{12,13},{14,15},{16,17},{18,... | collective-permute-start | bytes 73736 | tf_op jit(solution)/shard_map/ppermute | solution.py:16
  107.0 4.4 %collective-permute-start.9 = (f32[3,16,16,1]{3,2,1,0:T(8,128)}, f32[3,16,16,1]{3,2,1,0:T(8,128)}, u32[]{:S(2)}, u32[]{:S(2)}) collective-permute-start(f32[3,16,16,1]{3,2,1,0:T(8,128)} %get-tuple-element.151), channel_id=1, source_target_pairs={{2,0},{4,2},{6,4},{8,6},{10,8},{12,10},{14,12},{16,14},{18,16},{20... | collective-permute-start | bytes 9224 | tf_op jit(solution)/shard_map/ppermute | solution.py:19
  112.3 21.5 %all-gather.1 = f32[3,16,1,2048]{3,1,2,0:T(8,128)S(1)} all-gather(f32[3,16,1,128]{3,1,2,0:T(8,128)S(1)} %get-tuple-element.153), channel_id=3, replica_groups=mesh['lon'=16,'lat'=2] {'lon'}, dimensions={3}, use_global_device_ids=true | all-gather | bytes 417792 | tf_op jit(solution)/shard_map/all_gather | solution.py:74
  147.4 5.7 %collective-permute-start.14 = (f32[3,16,1,128]{3,1,0,2:T(8,128)}, f32[3,16,1,128]{3,1,0,2:T(8,128)}, u32[]{:S(2)}, u32[]{:S(2)}) collective-permute-start(f32[3,16,1,128]{3,1,0,2:T(8,128)} %get-tuple-element.150), channel_id=1, source_target_pairs={{0,1},{2,3},{4,5},{6,7},{8,9},{10,11},{12,13},{14,15},{16,17},{18,... | collective-permute-start | bytes 73736 | tf_op jit(solution)/shard_map/ppermute | solution.py:16
  154.5 4.4 %collective-permute-start.13 = (f32[3,16,16,1]{3,1,0,2:T(8,128)}, f32[3,16,16,1]{3,1,0,2:T(8,128)}, u32[]{:S(2)}, u32[]{:S(2)}) collective-permute-start(f32[3,16,16,1]{3,1,0,2:T(8,128)} %get-tuple-element.146), channel_id=1, source_target_pairs={{2,0},{4,2},{6,4},{8,6},{10,8},{12,10},{14,12},{16,14},{18,16},{20... | collective-permute-start | bytes 9224 | tf_op jit(solution)/shard_map/ppermute | solution.py:19
  158.9 23.7 %all-gather.2 = f32[3,16,1,2048]{3,1,2,0:T(8,128)} all-gather(f32[3,16,1,128]{3,1,2,0:T(8,128)S(1)} %get-tuple-element.148), channel_id=4, replica_groups=mesh['lon'=16,'lat'=2] {'lon'}, dimensions={3}, use_global_device_ids=true | all-gather | bytes 417792 | tf_op jit(solution)/shard_map/all_gather | solution.py:74
  182.6 4.4 %copy.585 = f32[3,16,1,2048]{1,0,3,2:T(4,128)} copy(f32[3,16,1,2048]{3,1,2,0:T(8,128)} %all-gather.2) | data formatting | bytes 786432 | tf_op jit(solution)/shard_map/all_gather | solution.py:74
  201.2 5.1 %collective-permute-start.18 = (f32[3,16,1,128]{3,1,0,2:T(8,128)}, f32[3,16,1,128]{3,1,0,2:T(8,128)S(1)}, u32[]{:S(2)}, u32[]{:S(2)}) collective-permute-start(f32[3,16,1,128]{3,1,0,2:T(8,128)} %get-tuple-element.145), channel_id=1, source_target_pairs={{0,1},{2,3},{4,5},{6,7},{8,9},{10,11},{12,13},{14,15},{16,17},{18,... | collective-permute-start | bytes 73736 | tf_op jit(solution)/shard_map/ppermute | solution.py:16
  207.8 4.4 %collective-permute-start.17 = (f32[3,16,16,1]{3,1,0,2:T(8,128)}, f32[3,16,16,1]{3,1,0,2:T(8,128)}, u32[]{:S(2)}, u32[]{:S(2)}) collective-permute-start(f32[3,16,16,1]{3,1,0,2:T(8,128)} %get-tuple-element.141), channel_id=1, source_target_pairs={{2,0},{4,2},{6,4},{8,6},{10,8},{12,10},{14,12},{16,14},{18,16},{20... | collective-permute-start | bytes 9224 | tf_op jit(solution)/shard_map/ppermute | solution.py:19
  212.1 23.7 %all-gather.3 = f32[3,16,1,2048]{3,1,2,0:T(8,128)} all-gather(f32[3,16,1,128]{3,1,2,0:T(8,128)S(1)} %get-tuple-element.143), channel_id=5, replica_groups=mesh['lon'=16,'lat'=2] {'lon'}, dimensions={3}, use_global_device_ids=true | all-gather | bytes 417792 | tf_op jit(solution)/shard_map/all_gather | solution.py:74
  235.8 4.4 %copy.597 = f32[3,16,1,2048]{1,0,3,2:T(4,128)} copy(f32[3,16,1,2048]{3,1,2,0:T(8,128)} %all-gather.3) | data formatting | bytes 786432 | tf_op jit(solution)/shard_map/all_gather | solution.py:74
  252.0 4.5 %collective-permute-start.22 = (f32[3,16,1,128]{3,1,0,2:T(8,128)S(1)}, f32[3,16,1,128]{3,1,0,2:T(8,128)S(1)}, u32[]{:S(2)}, u32[]{:S(2)}) collective-permute-start(f32[3,16,1,128]{3,1,0,2:T(8,128)S(1)} %get-tuple-element.138), channel_id=1, source_target_pairs={{0,1},{2,3},{4,5},{6,7},{8,9},{10,11},{12,13},{14,15},{16,17},{18,... | collective-permute-start | bytes 73736 | tf_op jit(solution)/shard_map/ppermute | solution.py:16
  258.0 4.4 %collective-permute-start.21 = (f32[3,16,16,1]{3,1,0,2:T(8,128)S(1)}, f32[3,16,16,1]{3,1,0,2:T(8,128)}, u32[]{:S(2)}, u32[]{:S(2)}) collective-permute-start(f32[3,16,16,1]{3,1,0,2:T(8,128)S(1)} %get-tuple-element.139), channel_id=1, source_target_pairs={{2,0},{4,2},{6,4},{8,6},{10,8},{12,10},{14,12},{16,14},{18,16},{20... | collective-permute-start | bytes 9224 | tf_op jit(solution)/shard_map/ppermute | solution.py:19
  262.4 22.0 %all-gather.4 = f32[3,16,1,2048]{3,1,2,0:T(8,128)S(1)} all-gather(f32[3,16,1,128]{3,1,2,0:T(8,128)S(1)} %get-tuple-element.137), channel_id=6, replica_groups=mesh['lon'=16,'lat'=2] {'lon'}, dimensions={3}, use_global_device_ids=true | all-gather | bytes 417792 | tf_op jit(solution)/shard_map/all_gather | solution.py:74
  296.5 4.5 %collective-permute-start.26 = (f32[3,16,1,128]{3,1,0,2:T(8,128)S(1)}, f32[3,16,1,128]{3,1,0,2:T(8,128)S(1)}, u32[]{:S(2)}, u32[]{:S(2)}) collective-permute-start(f32[3,16,1,128]{3,1,0,2:T(8,128)S(1)} %get-tuple-element.131), channel_id=1, source_target_pairs={{0,1},{2,3},{4,5},{6,7},{8,9},{10,11},{12,13},{14,15},{16,17},{18,... | collective-permute-start | bytes 73736 | tf_op jit(solution)/shard_map/ppermute | solution.py:16
  306.8 22.0 %all-gather.5 = f32[3,16,1,2048]{3,1,2,0:T(8,128)S(1)} all-gather(f32[3,16,1,128]{3,1,2,0:T(8,128)S(1)} %get-tuple-element.130), channel_id=7, replica_groups=mesh['lon'=16,'lat'=2] {'lon'}, dimensions={3}, use_global_device_ids=true | all-gather | bytes 417792 | tf_op jit(solution)/shard_map/all_gather | solution.py:74
  341.9 4.5 %collective-permute-start.30 = (f32[3,16,1,128]{3,1,0,2:T(8,128)S(1)}, f32[3,16,1,128]{3,1,0,2:T(8,128)S(1)}, u32[]{:S(2)}, u32[]{:S(2)}) collective-permute-start(f32[3,16,1,128]{3,1,0,2:T(8,128)S(1)} %get-tuple-element.121), channel_id=1, source_target_pairs={{0,1},{2,3},{4,5},{6,7},{8,9},{10,11},{12,13},{14,15},{16,17},{18,... | collective-permute-start | bytes 73736 | tf_op jit(solution)/shard_map/ppermute | solution.py:16
  347.9 4.4 %collective-permute-start.29 = (f32[3,16,16,1]{3,1,0,2:T(8,128)}, f32[3,16,16,1]{3,1,0,2:T(8,128)}, u32[]{:S(2)}, u32[]{:S(2)}) collective-permute-start(f32[3,16,16,1]{3,1,0,2:T(8,128)} %get-tuple-element.123), channel_id=1, source_target_pairs={{2,0},{4,2},{6,4},{8,6},{10,8},{12,10},{14,12},{16,14},{18,16},{20... | collective-permute-start | bytes 9224 | tf_op jit(solution)/shard_map/ppermute | solution.py:19
  352.3 22.2 %all-gather.6 = f32[3,16,1,2048]{3,1,2,0:T(8,128)S(1)} all-gather(f32[3,16,1,128]{3,1,2,0:T(8,128)S(1)} %get-tuple-element.120), channel_id=8, replica_groups=mesh['lon'=16,'lat'=2] {'lon'}, dimensions={3}, use_global_device_ids=true | all-gather | bytes 417792 | tf_op jit(solution)/shard_map/all_gather | solution.py:74
  387.2 38.1 %psum.7 = f32[]{:T(128)} all-reduce(f32[]{:T(128)} %get-tuple-element.93), channel_id=1, replica_groups=mesh['lon'=16,'lat'=2] {'lon','lat'}, use_global_device_ids=true, to_apply=%region_1.3 | all-reduce | flops 1 | bytes 8 | tf_op jit(solution)/shard_map/psum | solution.py:140
  (239 shorter events, 136.1 us)
Async XLA Ops:
  3.3 93.7 %collective-permute-start.6 = (f32[3,16,1,128]{3,1,0,2:T(8,128)}, f32[3,16,1,128]{3,1,0,2:T(8,128)}, u32[]{:S(2)}, u32[]{:S(2)}) collective-permute-start(f32[3,16,1,128]{3,1,0,2:T(8,128)} %get-tuple-element.160), channel_id=1, source_target_pairs={{0,1},{2,3},{4,5},{6,7},{8,9},{10,11},{12,13},{14,15},{16,17},{18,... | collective-permute-start | bytes 73736 | tf_op jit(solution)/shard_map/ppermute | solution.py:16
  8.8 88.2 %collective-permute-start.7 = (f32[3,16,1,128]{3,1,0,2:T(8,128)}, f32[3,16,1,128]{3,1,0,2:T(8,128)}, u32[]{:S(2)}, u32[]{:S(2)}) collective-permute-start(f32[3,16,1,128]{3,1,0,2:T(8,128)} %get-tuple-element.159), channel_id=1, source_target_pairs={{1,0},{3,2},{5,4},{7,6},{9,8},{11,10},{13,12},{15,14},{17,16},{19,... | collective-permute-start | bytes 73736 | tf_op jit(solution)/shard_map/ppermute | solution.py:19
  12.7 82.1 %collective-permute-start.5 = (f32[4,16,1,128]{3,2,1,0:T(1,128)}, f32[4,16,1,128]{3,2,1,0:T(1,128)}, u32[]{:S(2)}, u32[]{:S(2)}) collective-permute-start(f32[4,16,1,128]{3,2,1,0:T(1,128)} %get-tuple-element.119), channel_id=1, source_target_pairs={{1,0},{3,2},{5,4},{7,6},{9,8},{11,10},{13,12},{15,14},{17,16},{19,... | collective-permute-start | bytes 98312 | tf_op jit(solution)/shard_map/ppermute | solution.py:19
  15.2 63.2 %collective-permute-start.1 = (f32[4,16,16,1]{3,2,1,0:T(8,128)}, f32[4,16,16,1]{3,2,1,0:T(8,128)}, u32[]{:S(2)}, u32[]{:S(2)}) collective-permute-start(f32[4,16,16,1]{3,2,1,0:T(8,128)} %get-tuple-element.117), channel_id=1, source_target_pairs={{2,0},{4,2},{6,4},{8,6},{10,8},{12,10},{14,12},{16,14},{18,16},{20... | collective-permute-start | bytes 12296 | tf_op jit(solution)/shard_map/ppermute | solution.py:19
  18.9 59.8 %collective-permute-start = (f32[4,16,16,1]{3,2,1,0:T(8,128)}, f32[4,16,16,1]{3,2,1,0:T(8,128)}, u32[]{:S(2)}, u32[]{:S(2)}) collective-permute-start(f32[4,16,16,1]{3,2,1,0:T(8,128)} %get-tuple-element.116), channel_id=1, source_target_pairs={{0,2},{2,4},{4,6},{6,8},{8,10},{10,12},{12,14},{14,16},{16,18},{18... | collective-permute-start | bytes 12296 | tf_op jit(solution)/shard_map/ppermute | solution.py:16
  101.0 41.4 %collective-permute-start.10 = (f32[3,16,1,128]{3,1,0,2:T(8,128)}, f32[3,16,1,128]{3,1,0,2:T(8,128)}, u32[]{:S(2)}, u32[]{:S(2)}) collective-permute-start(f32[3,16,1,128]{3,1,0,2:T(8,128)} %get-tuple-element.155), channel_id=1, source_target_pairs={{0,1},{2,3},{4,5},{6,7},{8,9},{10,11},{12,13},{14,15},{16,17},{18,... | collective-permute-start | bytes 73736 | tf_op jit(solution)/shard_map/ppermute | solution.py:16
  105.7 36.6 %collective-permute-start.11 = (f32[3,16,1,128]{3,1,0,2:T(8,128)}, f32[3,16,1,128]{3,1,0,2:T(8,128)}, u32[]{:S(2)}, u32[]{:S(2)}) collective-permute-start(f32[3,16,1,128]{3,1,0,2:T(8,128)} %get-tuple-element.154), channel_id=1, source_target_pairs={{1,0},{3,2},{5,4},{7,6},{9,8},{11,10},{13,12},{15,14},{17,16},{19,... | collective-permute-start | bytes 73736 | tf_op jit(solution)/shard_map/ppermute | solution.py:19
  147.4 47.8 %collective-permute-start.14 = (f32[3,16,1,128]{3,1,0,2:T(8,128)}, f32[3,16,1,128]{3,1,0,2:T(8,128)}, u32[]{:S(2)}, u32[]{:S(2)}) collective-permute-start(f32[3,16,1,128]{3,1,0,2:T(8,128)} %get-tuple-element.150), channel_id=1, source_target_pairs={{0,1},{2,3},{4,5},{6,7},{8,9},{10,11},{12,13},{14,15},{16,17},{18,... | collective-permute-start | bytes 73736 | tf_op jit(solution)/shard_map/ppermute | solution.py:16
  153.1 42.1 %collective-permute-start.15 = (f32[3,16,1,128]{3,1,0,2:T(8,128)}, f32[3,16,1,128]{3,1,0,2:T(8,128)}, u32[]{:S(2)}, u32[]{:S(2)}) collective-permute-start(f32[3,16,1,128]{3,1,0,2:T(8,128)} %get-tuple-element.149), channel_id=1, source_target_pairs={{1,0},{3,2},{5,4},{7,6},{9,8},{11,10},{13,12},{15,14},{17,16},{19,... | collective-permute-start | bytes 73736 | tf_op jit(solution)/shard_map/ppermute | solution.py:19
  154.4 38.0 %collective-permute-start.12 = (f32[3,16,16,1]{3,1,0,2:T(8,128)}, f32[3,16,16,1]{3,1,0,2:T(8,128)}, u32[]{:S(2)}, u32[]{:S(2)}) collective-permute-start(f32[3,16,16,1]{3,1,0,2:T(8,128)} %get-tuple-element.147), channel_id=1, source_target_pairs={{0,2},{2,4},{4,6},{6,8},{8,10},{10,12},{12,14},{14,16},{16,18},{18... | collective-permute-start | bytes 9224 | tf_op jit(solution)/shard_map/ppermute | solution.py:16
  154.5 39.1 %collective-permute-start.13 = (f32[3,16,16,1]{3,1,0,2:T(8,128)}, f32[3,16,16,1]{3,1,0,2:T(8,128)}, u32[]{:S(2)}, u32[]{:S(2)}) collective-permute-start(f32[3,16,16,1]{3,1,0,2:T(8,128)} %get-tuple-element.146), channel_id=1, source_target_pairs={{2,0},{4,2},{6,4},{8,6},{10,8},{12,10},{14,12},{16,14},{18,16},{20... | collective-permute-start | bytes 9224 | tf_op jit(solution)/shard_map/ppermute | solution.py:19
  201.2 47.8 %collective-permute-start.18 = (f32[3,16,1,128]{3,1,0,2:T(8,128)}, f32[3,16,1,128]{3,1,0,2:T(8,128)S(1)}, u32[]{:S(2)}, u32[]{:S(2)}) collective-permute-start(f32[3,16,1,128]{3,1,0,2:T(8,128)} %get-tuple-element.145), channel_id=1, source_target_pairs={{0,1},{2,3},{4,5},{6,7},{8,9},{10,11},{12,13},{14,15},{16,17},{18,... | collective-permute-start | bytes 73736 | tf_op jit(solution)/shard_map/ppermute | solution.py:16
  206.3 42.7 %collective-permute-start.19 = (f32[3,16,1,128]{3,1,0,2:T(8,128)}, f32[3,16,1,128]{3,1,0,2:T(8,128)S(1)}, u32[]{:S(2)}, u32[]{:S(2)}) collective-permute-start(f32[3,16,1,128]{3,1,0,2:T(8,128)} %get-tuple-element.144), channel_id=1, source_target_pairs={{1,0},{3,2},{5,4},{7,6},{9,8},{11,10},{13,12},{15,14},{17,16},{19,... | collective-permute-start | bytes 73736 | tf_op jit(solution)/shard_map/ppermute | solution.py:19
  207.6 37.5 %collective-permute-start.16 = (f32[3,16,16,1]{3,1,0,2:T(8,128)}, f32[3,16,16,1]{3,1,0,2:T(8,128)}, u32[]{:S(2)}, u32[]{:S(2)}) collective-permute-start(f32[3,16,16,1]{3,1,0,2:T(8,128)} %get-tuple-element.142), channel_id=1, source_target_pairs={{0,2},{2,4},{4,6},{6,8},{8,10},{10,12},{12,14},{14,16},{16,18},{18... | collective-permute-start | bytes 9224 | tf_op jit(solution)/shard_map/ppermute | solution.py:16
  207.8 38.6 %collective-permute-start.17 = (f32[3,16,16,1]{3,1,0,2:T(8,128)}, f32[3,16,16,1]{3,1,0,2:T(8,128)}, u32[]{:S(2)}, u32[]{:S(2)}) collective-permute-start(f32[3,16,16,1]{3,1,0,2:T(8,128)} %get-tuple-element.141), channel_id=1, source_target_pairs={{2,0},{4,2},{6,4},{8,6},{10,8},{12,10},{14,12},{16,14},{18,16},{20... | collective-permute-start | bytes 9224 | tf_op jit(solution)/shard_map/ppermute | solution.py:19
  252.0 40.2 %collective-permute-start.22 = (f32[3,16,1,128]{3,1,0,2:T(8,128)S(1)}, f32[3,16,1,128]{3,1,0,2:T(8,128)S(1)}, u32[]{:S(2)}, u32[]{:S(2)}) collective-permute-start(f32[3,16,1,128]{3,1,0,2:T(8,128)S(1)} %get-tuple-element.138), channel_id=1, source_target_pairs={{0,1},{2,3},{4,5},{6,7},{8,9},{10,11},{12,13},{14,15},{16,17},{18,... | collective-permute-start | bytes 73736 | tf_op jit(solution)/shard_map/ppermute | solution.py:16
  256.6 35.7 %collective-permute-start.23 = (f32[3,16,1,128]{3,2,1,0:T(1,128)S(1)}, f32[3,16,1,128]{3,2,1,0:T(1,128)S(1)}, u32[]{:S(2)}, u32[]{:S(2)}) collective-permute-start(f32[3,16,1,128]{3,2,1,0:T(1,128)S(1)} %slice.756), channel_id=1, source_target_pairs={{1,0},{3,2},{5,4},{7,6},{9,8},{11,10},{13,12},{15,14},{17,16},{19,... | collective-permute-start | bytes 73736 | tf_op jit(solution)/shard_map/ppermute | solution.py:19
  296.5 41.6 %collective-permute-start.26 = (f32[3,16,1,128]{3,1,0,2:T(8,128)S(1)}, f32[3,16,1,128]{3,1,0,2:T(8,128)S(1)}, u32[]{:S(2)}, u32[]{:S(2)}) collective-permute-start(f32[3,16,1,128]{3,1,0,2:T(8,128)S(1)} %get-tuple-element.131), channel_id=1, source_target_pairs={{0,1},{2,3},{4,5},{6,7},{8,9},{10,11},{12,13},{14,15},{16,17},{18,... | collective-permute-start | bytes 73736 | tf_op jit(solution)/shard_map/ppermute | solution.py:16
  301.0 37.1 %collective-permute-start.27 = (f32[3,16,1,128]{3,1,0,2:T(8,128)S(1)}, f32[3,16,1,128]{3,1,0,2:T(8,128)S(1)}, u32[]{:S(2)}, u32[]{:S(2)}) collective-permute-start(f32[3,16,1,128]{3,1,0,2:T(8,128)S(1)} %get-tuple-element.132), channel_id=1, source_target_pairs={{1,0},{3,2},{5,4},{7,6},{9,8},{11,10},{13,12},{15,14},{17,16},{19,... | collective-permute-start | bytes 73736 | tf_op jit(solution)/shard_map/ppermute | solution.py:19
  302.3 34.4 %collective-permute-start.24 = (f32[3,16,16,1]{3,1,0,2:T(8,128)}, f32[3,16,16,1]{3,1,0,2:T(8,128)}, u32[]{:S(2)}, u32[]{:S(2)}) collective-permute-start(f32[3,16,16,1]{3,1,0,2:T(8,128)} %get-tuple-element.134), channel_id=1, source_target_pairs={{0,2},{2,4},{4,6},{6,8},{8,10},{10,12},{12,14},{14,16},{16,18},{18... | collective-permute-start | bytes 9224 | tf_op jit(solution)/shard_map/ppermute | solution.py:16
  341.9 41.9 %collective-permute-start.30 = (f32[3,16,1,128]{3,1,0,2:T(8,128)S(1)}, f32[3,16,1,128]{3,1,0,2:T(8,128)S(1)}, u32[]{:S(2)}, u32[]{:S(2)}) collective-permute-start(f32[3,16,1,128]{3,1,0,2:T(8,128)S(1)} %get-tuple-element.121), channel_id=1, source_target_pairs={{0,1},{2,3},{4,5},{6,7},{8,9},{10,11},{12,13},{14,15},{16,17},{18,... | collective-permute-start | bytes 73736 | tf_op jit(solution)/shard_map/ppermute | solution.py:16
  346.5 37.3 %collective-permute-start.31 = (f32[3,16,1,128]{3,1,0,2:T(8,128)S(1)}, f32[3,16,1,128]{3,1,0,2:T(8,128)S(1)}, u32[]{:S(2)}, u32[]{:S(2)}) collective-permute-start(f32[3,16,1,128]{3,1,0,2:T(8,128)S(1)} %get-tuple-element.122), channel_id=1, source_target_pairs={{1,0},{3,2},{5,4},{7,6},{9,8},{11,10},{13,12},{15,14},{17,16},{19,... | collective-permute-start | bytes 73736 | tf_op jit(solution)/shard_map/ppermute | solution.py:19
  347.8 34.6 %collective-permute-start.28 = (f32[3,16,16,1]{3,1,0,2:T(8,128)}, f32[3,16,16,1]{3,1,0,2:T(8,128)}, u32[]{:S(2)}, u32[]{:S(2)}) collective-permute-start(f32[3,16,16,1]{3,1,0,2:T(8,128)} %get-tuple-element.124), channel_id=1, source_target_pairs={{0,2},{2,4},{4,6},{6,8},{8,10},{10,12},{12,14},{14,16},{16,18},{18... | collective-permute-start | bytes 9224 | tf_op jit(solution)/shard_map/ppermute | solution.py:16
  347.9 34.5 %collective-permute-start.29 = (f32[3,16,16,1]{3,1,0,2:T(8,128)}, f32[3,16,16,1]{3,1,0,2:T(8,128)}, u32[]{:S(2)}, u32[]{:S(2)}) collective-permute-start(f32[3,16,16,1]{3,1,0,2:T(8,128)} %get-tuple-element.123), channel_id=1, source_target_pairs={{2,0},{4,2},{6,4},{8,6},{10,8},{12,10},{14,12},{16,14},{18,16},{20... | collective-permute-start | bytes 9224 | tf_op jit(solution)/shard_map/ppermute | solution.py:19
  (39 other events, 620.6 us)
where the time goes:
time: 430 us; the launch traced here: 427 us
  blocking collectives  216 us (50%)
  starting transfers between devices  85.6 us (20%)
  local copies, waits for them, and re-layouts  80.5 us (19%)
  other arithmetic  35.4 us (8%)
  waiting for transfers between devices  5.68 us (1%)
    all_gather x7, blocking collectives, neighbours(): whole_top = lax.all_gather(top_row, 'lon', axis=2, tiled=True)  155 us
    ppermute x16, starting transfers between devices, with_halo(): lax.ppermute(lax.slice_in_dim(block, 0, width, axis=dim), axis, backward)  44.4 us
    ppermute x16, starting transfers between devices, with_halo(): lax.ppermute(lax.slice_in_dim(block, block.shape[dim] - width, None, axis...  41.3 us
    psum x1, blocking collectives, on_device(): squares = lax.psum(jnp.sum(source_grad * source_grad), ('lon', 'lat'))  38.1 us
    gather x14, local copies, waits for them, and re-layouts, neighbours(): partner_row = jnp.take(whole_top, fold_partner, axis=2)  30 us
    all_gather x7, local copies, waits for them, and re-layouts, neighbours(): whole_top = lax.all_gather(top_row, 'lon', axis=2, tiled=True)  24.2 us
    all_gather x1, blocking collectives, on_device(): fold_all = lax.all_gather(top_static, 'lon', axis=2, tiled=True)  23.5 us
  transfers between devices with their start and end apart: 32, of which 2 were waited for; matrix products, arithmetic and copies ran while one was open for 20% of the time, Pallas kernels for 0%

commit v1 on v0

v1 whole, which is shorter than its diff:
```python
import functools

import jax
import jax.numpy as jnp
from jax import lax
from jax.experimental import pallas as pl
from jax.experimental.pallas import tpu as pltpu
from jax.sharding import PartitionSpec as P

STEPS = 4
UNROLL = 4
NEAR = (-1, 1, 2, 3)
F32 = jnp.float32


def upwind_pair(velocity, mixing, face_sea):
    flow_rate = velocity * face_sea
    mixing_part = mixing * face_sea
    return (jnp.maximum(flow_rate, 0.0) + mixing_part, jnp.minimum(flow_rate, 0.0) - mixing_part)


def kernel(
    lon_n,
    lat_n,
    start_ref,
    source_ref,
    target_ref,
    east_ref,
    north_ref,
    vert_ref,
    diff_ref,
    mask_ref,
    rate_ref,
    fold_ref,
    grad_ref,
    norm_ref,
    states,
    ocean_ref,
    cen,
    eo,
    en,
    wo,
    wn,
    no,
    nn,
    so,
    sn,
    uo,
    un,
    send_west,
    send_east,
    send_top,
    send_low,
    picked,
    got_lon,
    got_lat,
    got_far,
    got_near,
    sum_a,
    sum_b,
    sum_c,
    send_sem,
    recv_sem,
    sum_send,
    sum_recv,
):
    ntr, lev, rows, cols = start_ref.shape
    groups = lon_n // 4
    lon = lax.axis_index("lon")
    lat = lax.axis_index("lat")

    def at(lon_to, lat_to):
        return {"lon": lon_to, "lat": lat_to}

    def wrap(index, count):
        return lax.rem(index + 2 * count, count)

    low4 = lax.rem(lon, 4)
    high4 = lon // 4
    far = [wrap(4 * k - lon, lon_n) for k in range(groups)]

    from_ids = [(wrap(lon - 1, lon_n), lat), (wrap(lon + 1, lon_n), lat)]
    from_ids += [(lon, wrap(lat - 1, lat_n)), (lon, wrap(lat + 1, lat_n))]
    from_ids += [(wrap(lon - j, lon_n), lat) for j in NEAR]
    from_ids += [(high4 * 4 + wrap(low4 - j, 4), lat) for j in range(1, 4)]
    from_ids += [(wrap(lon - 4 * k, lon_n), lat) for k in range(1, groups)]
    from_ids += [(lon, wrap(lat - j, lat_n)) for j in range(1, lat_n)]
    barrier = pltpu.get_barrier_semaphore()
    for lon_from, lat_from in from_ids:
        pl.semaphore_signal(
            barrier, inc=1, device_id=at(lon_from, lat_from), device_id_type=pl.DeviceIdType.MESH
        )
    for k in range(groups):

        @pl.when(far[k] != lon)
        def _():
            pl.semaphore_signal(
                barrier, inc=1, device_id=at(far[k], lat), device_id_type=pl.DeviceIdType.MESH
            )

    peers = len(from_ids)
    for k in range(groups):
        peers = peers + (far[k] != lon).astype(jnp.int32)
    pl.semaphore_wait(barrier, peers)

    lane = lax.broadcasted_iota(jnp.int32, (rows, cols), 1)
    row = lax.broadcasted_iota(jnp.int32, (rows, cols), 0)
    is_top = (lat == lat_n - 1).astype(F32)
    not_top = 1.0 - is_top
    not_low = (lat != 0).astype(F32)

    lane1 = lax.broadcasted_iota(jnp.int32, (1, cols), 1)
    nx = lon_n * cols
    offset = fold_ref[...] + lane1 + lon * cols
    offset = jnp.where(offset >= nx, offset - nx, offset)
    offset = jnp.where(offset >= nx, offset - nx, offset)
    far_mask = []
    rest = offset
    for k in range(groups):
        inside = (offset >= 4 * k * cols) & (offset < 4 * (k + 1) * cols)
        far_mask.append(inside)
        rest = jnp.where(inside, offset - 4 * k * cols, rest)
    near_mask = []
    within = rest
    for j in range(4):
        inside = (rest >= j * cols) & (rest < (j + 1) * cols)
        near_mask.append(inside)
        within = jnp.where(inside, rest - j * cols, within)
    column = lax.broadcasted_iota(jnp.int32, (2 * cols, cols), 0)
    pick = (column == (within - lane1 + cols)).astype(F32)

    def remote(src, dst, e, slot, where):
        return pltpu.make_async_remote_copy(
            src_ref=src,
            dst_ref=dst,
            send_sem=send_sem.at[e, slot],
            recv_sem=recv_sem.at[e, slot],
            device_id=where,
            device_id_type=pl.DeviceIdType.MESH,
        )

    def sides(e):
        return [
            remote(send_east.at[e], got_lon.at[e, 0], e, 0, at(wrap(lon + 1, lon_n), lat)),
            remote(send_west.at[e], got_lon.at[e, 1], e, 1, at(wrap(lon - 1, lon_n), lat)),
            remote(send_top.at[e], got_lat.at[e, 0], e, 2, at(lon, wrap(lat + 1, lat_n))),
            remote(send_low.at[e], got_lat.at[e, 1], e, 3, at(lon, wrap(lat - 1, lat_n))),
        ]

    def far_copy(e, k):
        return remote(send_top.at[e], got_far.at[e, k], e, 8 + k, at(far[k], lat))

    def near_copies(e):
        return [
            remote(picked.at[e], got_near.at[e, i], e, 4 + i, at(wrap(lon + j, lon_n), lat))
            for i, j in enumerate(NEAR)
        ]

    def start(e, get_col, get_row):
        for t in range(ntr):
            send_top[e, pl.ds(t * lev, lev), :] = get_row(t, rows - 1)
            send_low[e, pl.ds(t * lev, lev), :] = get_row(t, 0)
        for k in range(groups):

            @pl.when(far[k] != lon)
            def _():
                far_copy(e, k).start()

            @pl.when(far[k] == lon)
            def _():
                got_far[e, k] = send_top[e]

        copies = sides(e)
        copies[2].start()
        copies[3].start()

        def body(level, carry):
            west, east = carry
            for t in range(ntr):
                value = get_col(t, level)
                here = lane == level + t * lev
                west = jnp.where(here, value[:, 0:1], west)
                east = jnp.where(here, value[:, cols - 1 : cols], east)
            return west, east

        blank = jnp.zeros((rows, cols), F32)
        west, east = lax.fori_loop(0, lev, body, (blank, blank), unroll=UNROLL)
        send_west[e] = west
        send_east[e] = east
        copies[0].start()
        copies[1].start()

    def fold_far(e):
        for k in range(groups):

            @pl.when(far[k] != lon)
            def _():
                far_copy(e, k).wait()

        chosen = got_far[e, 0]
        for k in range(1, groups):
            chosen = jnp.where(far_mask[k], got_far[e, k], chosen)
        picked[e] = chosen
        for copy in near_copies(e):
            copy.start()

    def fold_near(e):
        for copy in near_copies(e):
            copy.wait()
        by_shift = {0: picked[e]}
        for i, j in enumerate(NEAR):
            by_shift[j] = got_near[e, i]
        upper = by_shift[0]
        lower = by_shift[-1]
        for j in range(1, 4):
            upper = jnp.where(near_mask[j], by_shift[j], upper)
            lower = jnp.where(near_mask[j], by_shift[j - 1], lower)
        both = jnp.concatenate([lower, upper], axis=1)
        return jnp.dot(
            both, pick, preferred_element_type=F32, precision=lax.Precision.HIGHEST
        )

    def wait_sides(e):
        for copy in sides(e):
            copy.wait()

    def shift_lon(value, from_west, from_east):
        west = jnp.where(lane == 0, from_west, pltpu.roll(value, 1, 1))
        east = jnp.where(lane == cols - 1, from_east, pltpu.roll(value, cols - 1, 1))
        return west, east

    def shift_lat(value, from_south, from_north):
        south = jnp.where(row == 0, from_south, pltpu.roll(value, 1, 0))
        north = jnp.where(row == rows - 1, from_north, pltpu.roll(value, rows - 1, 0))
        return south, north

    ocean_ref[...] = mask_ref[...].astype(F32)
    east_set = (east_ref, diff_ref, ocean_ref)
    north_set = (north_ref, diff_ref, ocean_ref)
    start(0, lambda t, l: east_set[t][l], lambda t, r: north_set[t][:, r, :])
    start(1, lambda t, l: start_ref[t, l], lambda t, r: start_ref[t, :, r, :])
    fold_far(0)
    fold_far(1)
    wait_sides(0)
    across = fold_near(0)
    got_far[0, 0] = across

    uo[0] = jnp.zeros((rows, cols), F32)
    un[0] = jnp.zeros((rows, cols), F32)

    def coefficients(level, carry):
        west, east = carry
        above = jnp.minimum(level + 1, lev - 1)
        ev, nv, vv = east_ref[level], north_ref[level], vert_ref[level]
        d, o = diff_ref[level], ocean_ref[level]

        def lon_side(t):
            return west[:, t * lev : t * lev + 1], east[:, t * lev : t * lev + 1]

        def lat_row(side, t):
            return got_lat[0, side, pl.ds(t * lev + level, 1), :]

        def fold_row(t):
            return got_far[0, 0, pl.ds(t * lev + level, 1), :]

        ev_w, unused = shift_lon(ev, *lon_side(0))
        d_w, d_e = shift_lon(d, *lon_side(1))
        o_w, o_e = shift_lon(o, *lon_side(2))
        e_own, e_next = upwind_pair(ev, 0.5 * (d + d_e), o * o_e)
        w_own, w_next = upwind_pair(ev_w, 0.5 * (d_w + d), o_w * o)
        nv_s, unused = shift_lat(nv, lat_row(0, 0), lat_row(0, 0))
        d_s, d_n = shift_lat(d, lat_row(0, 1), not_top * lat_row(1, 1) + is_top * fold_row(1))
        o_s, o_n = shift_lat(
            o, not_low * lat_row(0, 2), not_top * lat_row(1, 2) + is_top * fold_row(2)
        )
        across_vel = is_top * (0.5 * (nv - fold_row(0))) + not_top * nv
        nq = jnp.where(row == rows - 1, across_vel, nv)
        n_own, n_next = upwind_pair(nq, 0.5 * (d + d_n), o * o_n)
        s_own, s_next = upwind_pair(nv_s, 0.5 * (d_s + d), o_s * o)
        inner = (level < lev - 1).astype(F32)
        u_own, u_next = upwind_pair(
            vv, 0.5 * (d + diff_ref[above]), o * ocean_ref[above] * inner
        )
        eo[level], en[level] = e_own, e_next
        wo[level], wn[level] = w_own, w_next
        no[level], nn[level] = n_own, n_next
        so[level], sn[level] = s_own, s_next
        uo[level + 1], un[level + 1] = u_own, u_next
        cen[level] = o - ((e_own - w_next) + (n_own - s_next) + (u_own - un[level]))
        return pltpu.roll(west, cols - 1, 1), pltpu.roll(east, cols - 1, 1)

    lax.fori_loop(0, lev, coefficients, (got_lon[0, 0], got_lon[0, 1]), unroll=UNROLL)

    last = 2 * STEPS - 2
    for step in range(last + 1):
        e = step + 1
        forward = step < STEPS
        src = start_ref if step == 0 else states.at[step - 1]
        dst = grad_ref if step == last else states.at[step]
        if step:
            fold_far(e)
        wait_sides(e)

        def advance(level, carry):
            west, east = carry
            above = jnp.minimum(level + 1, lev - 1)
            below = jnp.maximum(level - 1, 0)
            o = ocean_ref[level]
            middle = cen[level]
            if forward:
                k_e, k_w, k_n, k_s = en[level], wo[level], nn[level], so[level]
                k_u, k_d = un[level + 1], uo[level]
            else:
                k_e, k_w, k_n, k_s = eo[level], wn[level], no[level], sn[level]
                k_u, k_d = uo[level + 1], un[level]
            for t in range(ntr):
                value = src[t, level]
                v_w, v_e = shift_lon(
                    value, west[:, t * lev : t * lev + 1], east[:, t * lev : t * lev + 1]
                )
                v_s, v_n = shift_lat(
                    value,
                    got_lat[e, 0, pl.ds(t * lev + level, 1), :],
                    not_top * got_lat[e, 1, pl.ds(t * lev + level, 1), :],
                )
                v_u, v_d = src[t, above], src[t, below]
                out_flow = (k_e * v_e - k_w * v_w) + (k_n * v_n - k_s * v_s) + (k_u * v_u - k_d * v_d)
                rate = rate_ref[t, level]
                if forward:
                    root = lax.rsqrt(1.0 + value * value)
                    new = middle * value - out_flow + o * (
                        source_ref[t, level] - rate * (value * root)
                    )
                    if step == STEPS - 1:
                        new = new - o * target_ref[t, level]
                else:
                    state = states[2 * STEPS - 2 - step, t, level]
                    root = lax.rsqrt(1.0 + state * state)
                    new = middle * value + out_flow - rate * (root * root * root) * value
                    if step == last:
                        for other in range(STEPS - 1, last):
                            new = new + states[other, t, level]
                dst[t, level] = new
            return pltpu.roll(west, cols - 1, 1), pltpu.roll(east, cols - 1, 1)

        lax.fori_loop(0, lev, advance, (got_lon[e, 0], got_lon[e, 1]), unroll=UNROLL)
        across = fold_near(e)
        if forward:
            top_gain = -is_top * nn[:, rows - 1, :]
        else:
            top_gain = is_top * no[:, rows - 1, :]
        for t in range(ntr):
            dst[t, :, rows - 1, :] = (
                dst[t, :, rows - 1, :] + top_gain * across[t * lev : (t + 1) * lev, :]
            )
        if step < last:
            start(e + 1, lambda t, l: dst[t, l], lambda t, r: dst[t, :, r, :])

    def square(level, total):
        for t in range(ntr):
            value = grad_ref[t, level]
            total = total + value * value
        return total

    total = lax.fori_loop(0, lev, square, jnp.zeros((rows, cols), F32), unroll=UNROLL)

    def share(total, slots, mine, sem, targets):
        slots[mine] = total
        copies = [
            pltpu.make_async_remote_copy(
                src_ref=slots.at[mine],
                dst_ref=slots.at[mine],
                send_sem=sum_send.at[sem + i],
                recv_sem=sum_recv.at[sem + i],
                device_id=where,
                device_id_type=pl.DeviceIdType.MESH,
            )
            for i, where in enumerate(targets)
        ]
        for copy in copies:
            copy.start()
        for copy in copies:
            copy.wait()
        total = slots[0]
        for i in range(1, slots.shape[0]):
            total = total + slots[i]
        return total

    small = total[0:8]
    for r in range(8, rows, 8):
        small = small + total[r : r + 8]
    small = share(
        small, sum_a, low4, 0, [at(high4 * 4 + wrap(low4 + j, 4), lat) for j in range(1, 4)]
    )
    small = share(
        small, sum_b, high4, 3, [at(wrap(lon + 4 * k, lon_n), lat) for k in range(1, groups)]
    )
    small = share(
        small, sum_c, lat, 2 + groups, [at(lon, wrap(lat + j, lat_n)) for j in range(1, lat_n)]
    )
    norm_ref[...] = jnp.sqrt(jnp.sum(jnp.sum(small, axis=0, keepdims=True), axis=1, keepdims=True))


def on_device(lon_n, lat_n, *args):
    ntr, lev, rows, cols = args[0].shape
    fold = args[9].reshape(1, cols)
    groups = lon_n // 4
    exchanges = 2 * STEPS
    slots = 8 + groups
    vmem = pl.BlockSpec(memory_space=pltpu.VMEM)
    plane = pltpu.VMEM((lev, rows, cols), F32)
    tall = pltpu.VMEM((lev + 1, rows, cols), F32)
    column = pltpu.VMEM((exchanges, rows, cols), F32)
    line = pltpu.VMEM((exchanges, ntr * lev, cols), F32)
    grad, norm = pl.pallas_call(
        functools.partial(kernel, lon_n, lat_n),
        out_shape=(
            jax.ShapeDtypeStruct(args[0].shape, F32),
            jax.ShapeDtypeStruct((1, 1), F32),
        ),
        in_specs=[vmem] * 8 + [pl.BlockSpec(memory_space=pltpu.SMEM), vmem],
        out_specs=(vmem, vmem),
        scratch_shapes=[
            pltpu.VMEM((2 * STEPS - 2, ntr, lev, rows, cols), F32),
            plane,
            *[plane] * 9,
            tall,
            tall,
            column,
            column,
            line,
            line,
            line,
            pltpu.VMEM((exchanges, 2, rows, cols), F32),
            pltpu.VMEM((exchanges, 2, ntr * lev, cols), F32),
            pltpu.VMEM((exchanges, groups, ntr * lev, cols), F32),
            pltpu.VMEM((exchanges, len(NEAR), ntr * lev, cols), F32),
            pltpu.VMEM((4, 8, cols), F32),
            pltpu.VMEM((groups, 8, cols), F32),
            pltpu.VMEM((lat_n, 8, cols), F32),
            pltpu.SemaphoreType.DMA((exchanges, slots)),
            pltpu.SemaphoreType.DMA((exchanges, slots)),
            pltpu.SemaphoreType.DMA((2 + groups + lat_n,)),
            pltpu.SemaphoreType.DMA((2 + groups + lat_n,)),
        ],
        compiler_params=pltpu.CompilerParams(
            collective_id=0, has_side_effects=True, vmem_limit_bytes=40 * 1024 * 1024
        ),
    )(*args[:9], fold)
    return grad, norm[0, 0]


def solution(mesh):
    field = P(None, None, "lat", "lon")
    static = P(None, "lat", "lon")
    return jax.shard_map(
        functools.partial(on_device, mesh.shape["lon"], mesh.shape["lat"]),
        mesh=mesh,
        in_specs=(field, field, field, *[static] * 5, P(), P("lon")),
        out_specs=(field, P()),
        check_vma=False,
    )
```

time: 430 us -> 89.6 us (0.21)
  blocking collectives: 216 us -> 0 us
  starting transfers between devices: 85.6 us -> 0 us
  Pallas kernels: 0 us -> 77.2 us
  local copies, waits for them, and re-layouts: 80.5 us -> 9.58 us
  other arithmetic: 35.4 us -> 0 us
  waiting for transfers between devices: 5.68 us -> 0 us
    all_gather x8 -> x0, blocking collectives: 178 us -> none  [the longest x7 155 us: neighbours(): whole_top = lax.all_gather(top_row, 'lon', axis=2, tiled=True)]
    ppermute x32 -> x0, starting transfers between devices: 85.6 us -> none  [the longest x16 44.4 us: with_halo(): lax.ppermute(lax.slice_in_dim(block, 0, width, axis=dim), axis, backward)]
    pallas_call x0 -> x1, Pallas kernels: none -> 77.2 us  [on_device(): pl.pallas_call(functools.partial(kernel, lon_n, lat_n), out_shape=(jax.Sh...]
    psum x1 -> x0, blocking collectives: 38.1 us -> none  [on_device(): squares = lax.psum(jnp.sum(source_grad * source_grad), ('lon', 'lat'))]
    gather x16 -> x0, local copies, waits for them, and re-layouts: 33 us -> none  [the longest x14 30 us: neighbours(): partner_row = jnp.take(whole_top, fold_partner, axis=2)]
    all_gather x8 -> x0, local copies, waits for them, and re-layouts: 27.3 us -> none  [the longest x7 24.2 us: neighbours(): whole_top = lax.all_gather(top_row, 'lon', axis=2, tiled=True)]
    slice x30 -> x0, local copies, waits for them, and re-layouts: 12.1 us -> none  [the longest x8 6.95 us: with_halo(): lax.slice_in_dim(block, 0, width, axis=dim)]
    add x19 -> x0, other arithmetic: 10.7 us -> none  [the longest x4 3.37 us: on_device(): east_own * divergence_east_west[..., :-1]]
  transfers between devices with their start and end apart: 32 -> 0, of which waited for: 2 -> 0; matrix products, arithmetic and copies ran while one was open for 20% -> 0% of each run, Pallas kernels for 0% -> 0%
where the time goes in v1:
time: 89.6 us; the launch traced here: 89.3 us
  Pallas kernels  77.2 us (86%)
  local copies, waits for them, and re-layouts  9.58 us (11%)
  between operations  2.42 us (3%)
    pallas_call x1, Pallas kernels, on_device(): pl.pallas_call(functools.partial(kernel, lon_n, lat_n), out_shape=(jax.Sh...  77.2 us
    unnamed x21, local copies, waits for them, and re-layouts  9.58 us

profile of v1, /device:TPU:0, one launch (start us, length us, event | category | flops | bytes accessed | tf_op | source)
XLA Modules:
  0.0 89.3 jit_solution(16993019440912775575)
XLA Ops:
  0.6 0.0 copy-start.9
  0.6 0.6 copy-done.9
  1.3 0.0 copy-start
  1.3 1.0 %copy-done = f32[3,16,16,128]{3,2,1,0:T(8,128)S(1)} copy-done((f32[3,16,16,128]{3,2,1,0:T(8,128)S(1)}, f32[3,16,16,128]{3,2,1,0:T(8,128)}, u32[]{:S(2)}) %copy-start) | copy-done | bytes 393240
  2.3 0.0 copy-start.1
  2.3 1.0 %copy-done.1 = f32[3,16,16,128]{3,2,1,0:T(8,128)S(1)} copy-done((f32[3,16,16,128]{3,2,1,0:T(8,128)S(1)}, f32[3,16,16,128]{3,2,1,0:T(8,128)}, u32[]{:S(2)}) %copy-start.1) | copy-done | bytes 393240
  3.3 0.0 copy-start.2
  3.3 1.0 %copy-done.2 = f32[3,16,16,128]{3,2,1,0:T(8,128)S(1)} copy-done((f32[3,16,16,128]{3,2,1,0:T(8,128)S(1)}, f32[3,16,16,128]{3,2,1,0:T(8,128)}, u32[]{:S(2)}) %copy-start.2) | copy-done | bytes 393240
  4.3 0.0 copy-start.3
  4.3 0.9 %copy-done.3 = f32[16,16,128]{2,1,0:T(8,128)S(1)} copy-done((f32[16,16,128]{2,1,0:T(8,128)S(1)}, f32[16,16,128]{2,1,0:T(8,128)}, u32[]{:S(2)}) %copy-start.3) | copy-done | bytes 131096
  5.2 0.0 copy-start.4
  5.2 0.9 %copy-done.4 = f32[16,16,128]{2,1,0:T(8,128)S(1)} copy-done((f32[16,16,128]{2,1,0:T(8,128)S(1)}, f32[16,16,128]{2,1,0:T(8,128)}, u32[]{:S(2)}) %copy-start.4) | copy-done | bytes 131096
  6.1 0.0 copy-start.5
  6.1 0.9 %copy-done.5 = f32[16,16,128]{2,1,0:T(8,128)S(1)} copy-done((f32[16,16,128]{2,1,0:T(8,128)S(1)}, f32[16,16,128]{2,1,0:T(8,128)}, u32[]{:S(2)}) %copy-start.5) | copy-done | bytes 131096
  7.0 0.0 copy-start.6
  7.0 0.9 %copy-done.6 = f32[16,16,128]{2,1,0:T(8,128)S(1)} copy-done((f32[16,16,128]{2,1,0:T(8,128)S(1)}, f32[16,16,128]{2,1,0:T(8,128)}, u32[]{:S(2)}) %copy-start.6) | copy-done | bytes 131096
  7.9 0.0 copy-start.7
  7.9 0.9 %copy-done.7 = s32[16,16,128]{2,1,0:T(8,128)S(1)} copy-done((s32[16,16,128]{2,1,0:T(8,128)S(1)}, s32[16,16,128]{2,1,0:T(8,128)}, u32[]{:S(2)}) %copy-start.7) | copy-done | bytes 131096
  8.8 0.0 copy-start.8
  8.8 0.7 copy-done.8
  9.5 77.2 %shard_map.113 = (f32[3,16,16,128]{3,2,1,0:T(8,128)S(1)}, f32[1,1]{1,0:T(1,128)}) custom-call(f32[3,16,16,128]{3,2,1,0:T(8,128)S(1)} %copy-done, f32[3,16,16,128]{3,2,1,0:T(8,128)S(1)} %copy-done.1, f32[3,16,16,128]{3,2,1,0:T(8,128)S(1)} %copy-done.2, f32[16,16,128]{2,1,0:T(8,128)S(1)} %copy-done.3, f32[16,16,128]{2,1,0:T(8,128)S(1)} %copy-done.4, ...), custom_call_target="tpu_custom_call" | custom-call | tf_op jit(solution)/shard_map/pallas_call | solution.py:415
  86.7 0.7 copy.14
Async XLA Ops:
  0.6 0.7 copy-start.9
  1.3 1.0 %copy-start = (f32[3,16,16,128]{3,2,1,0:T(8,128)S(1)}, f32[3,16,16,128]{3,2,1,0:T(8,128)}, u32[]{:S(2)}) copy-start(f32[3,16,16,128]{3,2,1,0:T(8,128)} %start_ref.1) | copy-start | bytes 1179652
  2.3 1.0 %copy-start.1 = (f32[3,16,16,128]{3,2,1,0:T(8,128)S(1)}, f32[3,16,16,128]{3,2,1,0:T(8,128)}, u32[]{:S(2)}) copy-start(f32[3,16,16,128]{3,2,1,0:T(8,128)} %source_ref.1) | copy-start | bytes 1179652
  3.3 1.0 %copy-start.2 = (f32[3,16,16,128]{3,2,1,0:T(8,128)S(1)}, f32[3,16,16,128]{3,2,1,0:T(8,128)}, u32[]{:S(2)}) copy-start(f32[3,16,16,128]{3,2,1,0:T(8,128)} %target_ref.1) | copy-start | bytes 1179652
  4.3 0.9 %copy-start.3 = (f32[16,16,128]{2,1,0:T(8,128)S(1)}, f32[16,16,128]{2,1,0:T(8,128)}, u32[]{:S(2)}) copy-start(f32[16,16,128]{2,1,0:T(8,128)} %east_ref.1) | copy-start | bytes 393220
  5.2 0.9 %copy-start.4 = (f32[16,16,128]{2,1,0:T(8,128)S(1)}, f32[16,16,128]{2,1,0:T(8,128)}, u32[]{:S(2)}) copy-start(f32[16,16,128]{2,1,0:T(8,128)} %north_ref.1) | copy-start | bytes 393220
  6.1 0.9 %copy-start.5 = (f32[16,16,128]{2,1,0:T(8,128)S(1)}, f32[16,16,128]{2,1,0:T(8,128)}, u32[]{:S(2)}) copy-start(f32[16,16,128]{2,1,0:T(8,128)} %vert_ref.1) | copy-start | bytes 393220
  7.0 0.9 %copy-start.6 = (f32[16,16,128]{2,1,0:T(8,128)S(1)}, f32[16,16,128]{2,1,0:T(8,128)}, u32[]{:S(2)}) copy-start(f32[16,16,128]{2,1,0:T(8,128)} %diff_ref.1) | copy-start | bytes 393220
  7.9 0.9 %copy-start.7 = (s32[16,16,128]{2,1,0:T(8,128)S(1)}, s32[16,16,128]{2,1,0:T(8,128)}, u32[]{:S(2)}) copy-start(s32[16,16,128]{2,1,0:T(8,128)} %mask_ref.1) | copy-start | bytes 393220
  8.8 0.7 copy-start.8

commit v2 on v1

--- a/solution.py
+++ b/solution.py
@@ -22,6 +22,18 @@
 def kernel(
     lon_n,
     lat_n,
+    start_hbm,
+    source_hbm,
+    target_hbm,
+    east_hbm,
+    north_hbm,
+    vert_hbm,
+    diff_hbm,
+    mask_hbm,
+    rate_hbm,
+    fold_hbm,
+    grad_ref,
+    norm_ref,
     start_ref,
     source_ref,
     target_ref,
@@ -32,8 +44,7 @@
     mask_ref,
     rate_ref,
     fold_ref,
-    grad_ref,
-    norm_ref,
+    load_sem,
     states,
     ocean_ref,
     cen,
@@ -58,7 +69,6 @@
     got_near,
     sum_a,
     sum_b,
-    sum_c,
     send_sem,
     recv_sem,
     sum_send,
@@ -66,6 +76,24 @@
 ):
     ntr, lev, rows, cols = start_ref.shape
     groups = lon_n // 4
+    pairs = {
+        "mask": (mask_hbm, mask_ref),
+        "diff": (diff_hbm, diff_ref),
+        "north": (north_hbm, north_ref),
+        "east": (east_hbm, east_ref),
+        "start": (start_hbm, start_ref),
+        "fold": (fold_hbm, fold_ref),
+        "vert": (vert_hbm, vert_ref),
+        "rate": (rate_hbm, rate_ref),
+        "source": (source_hbm, source_ref),
+        "target": (target_hbm, target_ref),
+    }
+    loads = {
+        name: pltpu.make_async_copy(src, dst, load_sem.at[i])
+        for i, (name, (src, dst)) in enumerate(pairs.items())
+    }
+    for copy in loads.values():
+        copy.start()
     lon = lax.axis_index("lon")
     lat = lax.axis_index("lat")
 
@@ -82,9 +110,13 @@
     from_ids = [(wrap(lon - 1, lon_n), lat), (wrap(lon + 1, lon_n), lat)]
     from_ids += [(lon, wrap(lat - 1, lat_n)), (lon, wrap(lat + 1, lat_n))]
     from_ids += [(wrap(lon - j, lon_n), lat) for j in NEAR]
-    from_ids += [(high4 * 4 + wrap(low4 - j, 4), lat) for j in range(1, 4)]
+    from_ids += [
+        (high4 * 4 + wrap(low4 - j, 4), wrap(lat - i, lat_n))
+        for i in range(lat_n)
+        for j in range(4)
+        if i or j
+    ]
     from_ids += [(wrap(lon - 4 * k, lon_n), lat) for k in range(1, groups)]
-    from_ids += [(lon, wrap(lat - j, lat_n)) for j in range(1, lat_n)]
     barrier = pltpu.get_barrier_semaphore()
     for lon_from, lat_from in from_ids:
         pl.semaphore_signal(
@@ -109,6 +141,133 @@
     not_top = 1.0 - is_top
     not_low = (lat != 0).astype(F32)
 
+    def remote(src, dst, e, slot, where):
+        return pltpu.make_async_remote_copy(
+            src_ref=src,
+            dst_ref=dst,
+            send_sem=send_sem.at[e, slot],
+            recv_sem=recv_sem.at[e, slot],
+            device_id=where,
+            device_id_type=pl.DeviceIdType.MESH,
+        )
+
+    def sides(e):
+        return [
+            remote(send_east.at[e], got_lon.at[e, 0], e, 0, at(wrap(lon + 1, lon_n), lat)),
+            remote(send_west.at[e], got_lon.at[e, 1], e, 1, at(wrap(lon - 1, lon_n), lat)),
+            remote(send_top.at[e], got_lat.at[e, 0], e, 2, at(lon, wrap(lat + 1, lat_n))),
+            remote(send_low.at[e], got_lat.at[e, 1], e, 3, at(lon, wrap(lat - 1, lat_n))),
+        ]
+
+    def far_copy(e, k):
+        return remote(send_top.at[e], got_far.at[e, k], e, 8 + k, at(far[k], lat))
+
+    def near_copies(e):
+        return [
+            remote(picked.at[e], got_near.at[e, i], e, 4 + i, at(wrap(lon + j, lon_n), lat))
+            for i, j in enumerate(NEAR)
+        ]
+
+    def send_tops(e):
+        for k in range(groups):
+
+            @pl.when(far[k] != lon)
+            def _():
+                far_copy(e, k).start()
+
+            @pl.when(far[k] == lon)
+            def _():
+                got_far[e, k] = send_top[e]
+
+        sides(e)[2].start()
+
+    def send_lows(e):
+        sides(e)[3].start()
+
+    def send_columns(e, get_col):
+        def body(level, carry):
+            west, east = carry
+            for t in range(ntr):
+                value = get_col(t, level)
+                here = lane == level + t * lev
+                west = jnp.where(here, value[:, 0:1], west)
+                east = jnp.where(here, value[:, cols - 1 : cols], east)
+            return west, east
+
+        blank = jnp.zeros((rows, cols), F32)
+        west, east = lax.fori_loop(0, lev, body, (blank, blank), unroll=UNROLL)
+        send_west[e] = west
+        send_east[e] = east
+        sides(e)[0].start()
+        sides(e)[1].start()
+
+    def start(e, get_col, get_row):
+        for t in range(ntr):
+            send_top[e, pl.ds(t * lev, lev), :] = get_row(t, rows - 1)
+        send_tops(e)
+        for t in range(ntr):
+            send_low[e, pl.ds(t * lev, lev), :] = get_row(t, 0)
+        send_lows(e)
+        send_columns(e, get_col)
+
+    def fold_far(e):
+        for k in range(groups):
+
+            @pl.when(far[k] != lon)
+            def _():
+                far_copy(e, k).wait()
+
+        chosen = got_far[e, 0]
+        for k in range(1, groups):
+            chosen = jnp.where(far_mask[k], got_far[e, k], chosen)
+        picked[e] = chosen
+        for copy in near_copies(e):
+            copy.start()
+
+    def fold_near(e):
+        for copy in near_copies(e):
+            copy.wait()
+        by_shift = {0: picked[e]}
+        for i, j in enumerate(NEAR):
+            by_shift[j] = got_near[e, i]
+        upper = by_shift[0]
+        lower = by_shift[-1]
+        for j in range(1, 4):
+            upper = jnp.where(near_mask[j], by_shift[j], upper)
+            lower = jnp.where(near_mask[j], by_shift[j - 1], lower)
+        both = jnp.concatenate([lower, upper], axis=1)
+        high = both.astype(jnp.bfloat16)
+        rest1 = both - high.astype(F32)
+        mid = rest1.astype(jnp.bfloat16)
+        low = (rest1 - mid.astype(F32)).astype(jnp.bfloat16)
+        parts = jnp.concatenate([high, mid, low], axis=0)
+        found = jnp.dot(parts, pick, preferred_element_type=F32)
+        count = ntr * lev
+        return found[0:count] + found[count : 2 * count] + found[2 * count :]
+
+    def wait_sides(e):
+        for copy in sides(e):
+            copy.wait()
+
+    def shift_lon(value, from_west, from_east):
+        west = jnp.where(lane == 0, from_west, pltpu.roll(value, 1, 1))
+        east = jnp.where(lane == cols - 1, from_east, pltpu.roll(value, cols - 1, 1))
+        return west, east
+
+    def shift_lat(value, from_south, from_north):
+        south = jnp.where(row == 0, from_south, pltpu.roll(value, 1, 0))
+        north = jnp.where(row == rows - 1, from_north, pltpu.roll(value, rows - 1, 0))
+        return south, north
+
+    for name in ("mask", "diff", "north", "east"):
+        loads[name].wait()
+    ocean_ref[...] = mask_ref[...].astype(F32)
+    east_set = (east_ref, diff_ref, ocean_ref)
+    north_set = (north_ref, diff_ref, ocean_ref)
+    start(0, lambda t, l: east_set[t][l], lambda t, r: north_set[t][:, r, :])
+    loads["start"].wait()
+    start(1, lambda t, l: start_ref[t, l], lambda t, r: start_ref[t, :, r, :])
+    loads["fold"].wait()
     lane1 = lax.broadcasted_iota(jnp.int32, (1, cols), 1)
     nx = lon_n * cols
     offset = fold_ref[...] + lane1 + lon * cols
@@ -127,118 +286,10 @@
         near_mask.append(inside)
         within = jnp.where(inside, rest - j * cols, within)
     column = lax.broadcasted_iota(jnp.int32, (2 * cols, cols), 0)
-    pick = (column == (within - lane1 + cols)).astype(F32)
-
-    def remote(src, dst, e, slot, where):
-        return pltpu.make_async_remote_copy(
-            src_ref=src,
-            dst_ref=dst,
-            send_sem=send_sem.at[e, slot],
-            recv_sem=recv_sem.at[e, slot],
-            device_id=where,
-            device_id_type=pl.DeviceIdType.MESH,
-        )
-
-    def sides(e):
-        return [
-            remote(send_east.at[e], got_lon.at[e, 0], e, 0, at(wrap(lon + 1, lon_n), lat)),
-            remote(send_west.at[e], got_lon.at[e, 1], e, 1, at(wrap(lon - 1, lon_n), lat)),
-            remote(send_top.at[e], got_lat.at[e, 0], e, 2, at(lon, wrap(lat + 1, lat_n))),
-            remote(send_low.at[e], got_lat.at[e, 1], e, 3, at(lon, wrap(lat - 1, lat_n))),
-        ]
-
-    def far_copy(e, k):
-        return remote(send_top.at[e], got_far.at[e, k], e, 8 + k, at(far[k], lat))
-
-    def near_copies(e):
-        return [
-            remote(picked.at[e], got_near.at[e, i], e, 4 + i, at(wrap(lon + j, lon_n), lat))
-            for i, j in enumerate(NEAR)
-        ]
-
-    def start(e, get_col, get_row):
-        for t in range(ntr):
-            send_top[e, pl.ds(t * lev, lev), :] = get_row(t, rows - 1)
-            send_low[e, pl.ds(t * lev, lev), :] = get_row(t, 0)
-        for k in range(groups):
-
-            @pl.when(far[k] != lon)
-            def _():
-                far_copy(e, k).start()
-
-            @pl.when(far[k] == lon)
-            def _():
-                got_far[e, k] = send_top[e]
-
-        copies = sides(e)
-        copies[2].start()
-        copies[3].start()
-
-        def body(level, carry):
-            west, east = carry
-            for t in range(ntr):
-                value = get_col(t, level)
-                here = lane == level + t * lev
-                west = jnp.where(here, value[:, 0:1], west)
-                east = jnp.where(here, value[:, cols - 1 : cols], east)
-            return west, east
-
-        blank = jnp.zeros((rows, cols), F32)
-        west, east = lax.fori_loop(0, lev, body, (blank, blank), unroll=UNROLL)
-        send_west[e] = west
-        send_east[e] = east
-        copies[0].start()
-        copies[1].start()
-
-    def fold_far(e):
-        for k in range(groups):
-
-            @pl.when(far[k] != lon)
-            def _():
-                far_copy(e, k).wait()
-
-        chosen = got_far[e, 0]
-        for k in range(1, groups):
-            chosen = jnp.where(far_mask[k], got_far[e, k], chosen)
-        picked[e] = chosen
-        for copy in near_copies(e):
-            copy.start()
-
-    def fold_near(e):
-        for copy in near_copies(e):
-            copy.wait()
-        by_shift = {0: picked[e]}
-        for i, j in enumerate(NEAR):
-            by_shift[j] = got_near[e, i]
-        upper = by_shift[0]
-        lower = by_shift[-1]
-        for j in range(1, 4):
-            upper = jnp.where(near_mask[j], by_shift[j], upper)
-            lower = jnp.where(near_mask[j], by_shift[j - 1], lower)
-        both = jnp.concatenate([lower, upper], axis=1)
-        return jnp.dot(
-            both, pick, preferred_element_type=F32, precision=lax.Precision.HIGHEST
-        )
-
-    def wait_sides(e):
-        for copy in sides(e):
-            copy.wait()
-
-    def shift_lon(value, from_west, from_east):
-        west = jnp.where(lane == 0, from_west, pltpu.roll(value, 1, 1))
-        east = jnp.where(lane == cols - 1, from_east, pltpu.roll(value, cols - 1, 1))
-        return west, east
-
-    def shift_lat(value, from_south, from_north):
-        south = jnp.where(row == 0, from_south, pltpu.roll(value, 1, 0))
-        north = jnp.where(row == rows - 1, from_north, pltpu.roll(value, rows - 1, 0))
-        return south, north
-
-    ocean_ref[...] = mask_ref[...].astype(F32)
-    east_set = (east_ref, diff_ref, ocean_ref)
-    north_set = (north_ref, diff_ref, ocean_ref)
-    start(0, lambda t, l: east_set[t][l], lambda t, r: north_set[t][:, r, :])
-    start(1, lambda t, l: start_ref[t, l], lambda t, r: start_ref[t, :, r, :])
+    pick = (column == (within - lane1 + cols)).astype(F32).astype(jnp.bfloat16)
+
+    for name in ("vert", "rate", "source", "target"):
+        loads[name].wait()
     fold_far(0)
     fold_far(1)
     wait_sides(0)
@@ -344,17 +395,27 @@
             return pltpu.roll(west, cols - 1, 1), pltpu.roll(east, cols - 1, 1)
 
         lax.fori_loop(0, lev, advance, (got_lon[e, 0], got_lon[e, 1]), unroll=UNROLL)
+        if step < last:
+            for t in range(ntr):
+                send_low[e + 1, pl.ds(t * lev, lev), :] = dst[t, :, 0, :]
+            send_lows(e + 1)
         across = fold_near(e)
         if forward:
             top_gain = -is_top * nn[:, rows - 1, :]
         else:
             top_gain = is_top * no[:, rows - 1, :]
+        tops = [
+            dst[t, :, rows - 1, :] + top_gain * across[t * lev : (t + 1) * lev, :]
+            for t in range(ntr)
+        ]
+        if step < last:
+            for t in range(ntr):
+                send_top[e + 1, pl.ds(t * lev, lev), :] = tops[t]
+            send_tops(e + 1)
         for t in range(ntr):
-            dst[t, :, rows - 1, :] = (
-                dst[t, :, rows - 1, :] + top_gain * across[t * lev : (t + 1) * lev, :]
-            )
+            dst[t, :, rows - 1, :] = tops[t]
         if step < last:
-            start(e + 1, lambda t, l: dst[t, l], lambda t, r: dst[t, :, r, :])
+            send_columns(e + 1, lambda t, l: dst[t, l])
 
     def square(level, total):
         for t in range(ntr):
@@ -389,15 +450,15 @@
     small = total[0:8]
     for r in range(8, rows, 8):
         small = small + total[r : r + 8]
-    small = share(
-        small, sum_a, low4, 0, [at(high4 * 4 + wrap(low4 + j, 4), lat) for j in range(1, 4)]
-    )
-    small = share(
-        small, sum_b, high4, 3, [at(wrap(lon + 4 * k, lon_n), lat) for k in range(1, groups)]
-    )
-    small = share(
-        small, sum_c, lat, 2 + groups, [at(lon, wrap(lat + j, lat_n)) for j in range(1, lat_n)]
-    )
+    near_ids = [
+        at(high4 * 4 + wrap(low4 + j, 4), wrap(lat + i, lat_n))
+        for i in range(lat_n)
+        for j in range(4)
+        if i or j
+    ]
+    far_ids = [at(wrap(lon + 4 * k, lon_n), lat) for k in range(1, groups)]
+    small = share(small, sum_a, lat * 4 + low4, 0, near_ids)
+    small = share(small, sum_b, high4, len(near_ids), far_ids)
     norm_ref[...] = jnp.sqrt(jnp.sum(jnp.sum(small, axis=0, keepdims=True), axis=1, keepdims=True))
 
 
@@ -418,9 +479,13 @@
             jax.ShapeDtypeStruct(args[0].shape, F32),
             jax.ShapeDtypeStruct((1, 1), F32),
         ),
-        in_specs=[vmem] * 8 + [pl.BlockSpec(memory_space=pltpu.SMEM), vmem],
+        in_specs=[pl.BlockSpec(memory_space=pltpu.HBM)] * 10,
         out_specs=(vmem, vmem),
         scratch_shapes=[
+            *[pltpu.VMEM(a.shape, a.dtype) for a in args[:8]],
+            pltpu.SMEM(args[8].shape, F32),
+            pltpu.VMEM(fold.shape, jnp.int32),
+            pltpu.SemaphoreType.DMA((10,)),
             pltpu.VMEM((2 * STEPS - 2, ntr, lev, rows, cols), F32),
             plane,
             *[plane] * 9,
@@ -435,16 +500,15 @@
             pltpu.VMEM((exchanges, 2, ntr * lev, cols), F32),
             pltpu.VMEM((exchanges, groups, ntr * lev, cols), F32),
             pltpu.VMEM((exchanges, len(NEAR), ntr * lev, cols), F32),
-            pltpu.VMEM((4, 8, cols), F32),
+            pltpu.VMEM((4 * lat_n, 8, cols), F32),
             pltpu.VMEM((groups, 8, cols), F32),
-            pltpu.VMEM((lat_n, 8, cols), F32),
             pltpu.SemaphoreType.DMA((exchanges, slots)),
             pltpu.SemaphoreType.DMA((exchanges, slots)),
-            pltpu.SemaphoreType.DMA((2 + groups + lat_n,)),
-            pltpu.SemaphoreType.DMA((2 + groups + lat_n,)),
+            pltpu.SemaphoreType.DMA((4 * lat_n + groups,)),
+            pltpu.SemaphoreType.DMA((4 * lat_n + groups,)),
         ],
         compiler_params=pltpu.CompilerParams(
-            collective_id=0, has_side_effects=True, vmem_limit_bytes=40 * 1024 * 1024
+            collective_id=0, has_side_effects=True, vmem_limit_bytes=64 * 1024 * 1024 - 65536
         ),
     )(*args[:9], fold)
     return grad, norm[0, 0]

time: 89.6 us -> 79.2 us (0.88)
  local copies, waits for them, and re-layouts: 9.58 us -> 1.77 us
  Pallas kernels: 77.2 us -> 74.9 us
    unnamed x21 -> x1, local copies, waits for them, and re-layouts: 9.58 us -> 1.77 us
    pallas_call x1, Pallas kernels: 77.2 us -> 74.9 us  [on_device(): pl.pallas_call(functools.partial(kernel, lon_n, lat_n), out_shape=(jax.Sh...]
where the time goes in v2:
time: 79.2 us; the launch traced here: 79 us
  Pallas kernels  74.9 us (95%)
  between operations  2.4 us (3%)
  local copies, waits for them, and re-layouts  1.77 us (2%)
    pallas_call x1, Pallas kernels, on_device(): pl.pallas_call(functools.partial(kernel, lon_n, lat_n), out_shape=(jax.Sh...  74.9 us
    unnamed x1, local copies, waits for them, and re-layouts  1.77 us

profile of v2, /device:TPU:0, one launch (start us, length us, event | category | flops | bytes accessed | tf_op | source)
XLA Modules:
  0.0 79.0 jit_solution(10158076773935933904)
XLA Ops:
  0.6 74.9 %shard_map.113 = (f32[3,16,16,128]{3,2,1,0:T(8,128)}, f32[1,1]{1,0:T(1,128)}) custom-call(f32[3,16,16,128]{3,2,1,0:T(8,128)} %start_hbm.1, f32[3,16,16,128]{3,2,1,0:T(8,128)} %source_hbm.1, f32[3,16,16,128]{3,2,1,0:T(8,128)} %target_hbm.1, f32[16,16,128]{2,1,0:T(8,128)} %east_hbm.1, f32[16,16,128]{2,1,0:T(8,128)} %north_hbm.1, f32[16,16,128]{2,1,0:T(8,128)} %vert_hbm.1, ...), custom_call_target="tpu_custom_call" | custom-call | tf_op jit(solution)/shard_map/pallas_call | solution.py:476
  75.5 1.8 %copy.14 = f32[3,16,16,128]{3,2,1,0:T(8,128)} copy(f32[3,16,16,128]{3,2,1,0:T(8,128)} %get-tuple-element.8) | data formatting | bytes 786432
